TPU v7x, 512 devices: a whole 4x8x8 slice. The times are simulated.
512 devices in a mesh: layer: 16 (over x_lo, z), feat: 32 (over x_hi, y, core).
Axes of the slice: x: 4 (x_hi: 2, x_lo: 2; x = x_hi * 2 + x_lo), y: 8, z: 8, core: 2. Of those that a mesh axis runs over, the one named last changes fastest.
Arguments:
- grads: bfloat16 [2, 16, 256, 8192], P(None, 'layer', 'feat'), may hold values from -6 to 6
- decoder: bfloat16 [2, 16, 3072, 8192], P(None, 'layer', 'feat'), may hold values from -0.01171875 to 0.01171875
- active_ids: int32 [256, 128], replicated, may hold values from 0 to 3071, all different within a row
- act_vals: float32 [256, 128], P('layer'), may hold values from 0.2 to 2
Outputs:
- edges: float32 [256, 128], P('layer')
Inputs may be any that keep to these rules, and one draw needn't show every extreme that they name: `active_ids`: each row names 128 different features; every feature is named by some row; a few features are named far more often than others.
All inputs are finite; a program needn't handle non-finite values.
Results may differ from a plain program's by a relative error of at most 0.0003.
Values may be sent and summed in bfloat16 or wider, within the bound.
A program may use at most 64 MiB of HBM per device.

v0:
```python
import jax
import jax.numpy as jnp
from jax import lax
from jax.sharding import PartitionSpec as P


def select_owned(matrix, ids, shard_start):
    width = matrix.shape[1]
    local = ids - shard_start
    inside = jnp.logical_and(local >= 0, local < width)
    safe = jnp.clip(local, 0, width - 1)
    values = jnp.take_along_axis(matrix, safe, axis=1)
    return jnp.where(inside, values, jnp.float32(0.0))


def finish_scores(partial_scores, active_ids, shard_start, block_start, block_rows):
    block_scores = lax.psum_scatter(partial_scores, "layer", scatter_dimension=0, tiled=True)
    block_ids = lax.dynamic_slice_in_dim(active_ids, block_start, block_rows, 0)
    owned = select_owned(block_scores, block_ids, shard_start)
    return lax.psum(owned, "feat")


def shards(grads, decoder, active_ids, act_vals):
    grad_pair = grads[:, 0]
    dec_pair = decoder[:, 0]
    feat_count = dec_pair.shape[1]
    shard_start = lax.axis_index("feat") * feat_count
    block_rows = act_vals.shape[0]
    block_start = lax.axis_index("layer") * block_rows
    partial_scores = jnp.einsum(
        "ptd,pfd->tf",
        lax.all_gather(grad_pair, "feat", axis=1, tiled=True),
        dec_pair,
        preferred_element_type=jnp.float32,
    )
    picked = finish_scores(partial_scores, active_ids, shard_start, block_start, block_rows)
    return act_vals * picked


def solution(mesh):
    placed = (P(None, "layer", "feat", None), P(None, "layer", "feat", None), P(), P("layer", None))
    return jax.shard_map(
        shards, mesh=mesh, in_specs=placed, out_specs=P("layer", None), check_vma=False
    )
```

profile of v0, /device:TPU:1, one launch (start us, length us, event | category | flops | bytes accessed | tf_op | source)
XLA Modules:
  0.0 287.5 jit_solution(671437815956423548)
XLA Ops:
  6.5 0.0 copy-start
  6.5 0.0 all-gather.3.cloned.1.call-start
  6.5 0.7 all-gather.3.cloned.1.call-update
  7.3 0.0 copy-start.1
  7.3 0.0 reduce-scatter.2.cloned.1.call-start
  7.3 116.1 %all-gather.3.cloned.1.call-done = bf16[2,1,256,8192]{3,2,0,1:T(8,128)(2,1)} async-done(((bf16[2,1,8,8192]{3,2,0,1:T(8,128)(2,1)}), bf16[2,1,256,8192]{3,2,0,1:T(8,128)(2,1)}) %all-gather.3.cloned.1.call-update) | async-done | bytes 8388624 | tf_op jit(solution)/shard_map/all_gather | solution.py:32
  123.4 0.0 copy-done
  123.4 6.4 %fusion.3 = f32[256,96]{1,0:T(8,128)} fusion(bf16[2,1,96,8192]{3,2,1,0:T(8,128)(2,1)S(1)} %copy-done, bf16[2,1,256,8192]{3,2,0,1:T(8,128)(2,1)} %all-gather.3.cloned.1.call-done), kind=kOutput, calls=%fused_computation.4 | convolution fusion | flops 805306368 | bytes 11632640 | tf_op jit(solution)/shard_map/ptd,pfd->tf/dot_general | solution.py:30
  129.8 0.0 reduce-scatter.2.cloned.1.call-update
  129.8 0.7 fusion.9
  130.5 57.1 %reduce-scatter.2.cloned.1.call-done = f32[16,96]{1,0:T(8,128)} async-done(((f32[256,96]{1,0:T(8,128)}), f32[16,96]{1,0:T(8,128)}) %reduce-scatter.2.cloned.1.call-update) | async-done | bytes 6160 | tf_op jit(solution)/shard_map/reduce_scatter | solution.py:17
  187.6 13.8 %gather_fusion = f32[2048]{0:T(1024)S(1)} fusion(f32[16,96]{1,0:T(8,128)} %reduce-scatter.2.cloned.1.call-done, s32[2048]{0:T(1024)S(1)} %fusion.9), kind=kCustom, calls=%fused_computation | custom fusion | bytes 32768 | tf_op jit(solution)/shard_map/jit(take_along_axis)/gather | solution.py:12
  201.4 0.7 fusion.8
  202.1 77.9 %psum.7 = f32[16,128]{1,0:T(8,128)S(1)} all-reduce(f32[16,128]{1,0:T(8,128)S(1)} %fusion.8), channel_id=1, replica_groups=mesh['layer'=16,'feat'=32] {'feat'}, use_global_device_ids=true, to_apply=%region_1.2 | all-reduce | flops 2048 | bytes 16384 | tf_op jit(solution)/shard_map/psum | solution.py:20
  280.0 0.0 copy-done.1
  280.0 0.6 mul.11
Async XLA Ops:
  6.5 116.9 %copy-start = (bf16[2,1,96,8192]{3,2,1,0:T(8,128)(2,1)S(1)}, bf16[2,1,96,8192]{3,2,1,0:T(8,128)(2,1)}, u32[]{:S(2)}) copy-start(bf16[2,1,96,8192]{3,2,1,0:T(8,128)(2,1)} %param.5) | copy-start | bytes 9437188
  6.5 116.9 %all-gather.3.cloned.1.call-start = ((), (), s32[]{:S(2)}) async-start(), calls=%async_computation.2 | async-start | bytes 8650752 | tf_op jit(solution)/shard_map/all_gather | solution.py:32
  7.3 272.7 %copy-start.1 = (f32[16,128]{1,0:T(8,128)S(1)}, f32[16,128]{1,0:T(8,128)}, u32[]{:S(2)}) copy-start(f32[16,128]{1,0:T(8,128)} %param.7) | copy-start | bytes 24580
  7.3 180.3 %reduce-scatter.2.cloned.1.call-start = ((), (), s32[]{:S(2)}) async-start(), calls=%async_computation.1 | async-start | bytes 139264 | tf_op jit(solution)/shard_map/reduce_scatter | solution.py:17
Sparse Core Ops, SparseCore 0:
  10.8 112.5 all-gather.2
  129.9 57.6 reduce-scatter.1
where the time goes:
time: 288 us; the launch traced here: 287 us
  waiting for transfers between devices  174 us (60%)
  blocking collectives  77.9 us (27%)
  local copies, waits for them, and re-layouts  13.8 us (5%)
  between operations  13.4 us (5%)
  matrix products  6.37 us (2%)
    all_gather x1, waiting for transfers between devices, shards(): lax.all_gather(grad_pair, 'feat', axis=1, tiled=True)  116 us
    psum x1, blocking collectives, finish_scores(): return lax.psum(owned, 'feat')  77.9 us
    reduce_scatter x1, waiting for transfers between devices, finish_scores(): lax.psum_scatter(partial_scores, 'layer', scatter_dimension=0, tiled=True)  57.1 us
    gather x1, local copies, waits for them, and re-layouts, select_owned(): values = jnp.take_along_axis(matrix, safe, axis=1)  13.8 us
    dot_general x1, matrix products, shards(): jnp.einsum('ptd,pfd->tf', lax.all_gather(grad_pair, 'feat', axis=1, tiled...  6.37 us
  transfers between devices with their start and end apart: 2, of which 2 were waited for; matrix products, arithmetic and copies ran while one was open for 0% of the time, Pallas kernels for 0%

commit v1 on v0

v1 whole, which is shorter than its diff:
```python
import functools

import jax
import jax.numpy as jnp
from jax import lax
from jax.experimental import pallas as pl
from jax.experimental.pallas import tpu as pltpu
from jax.sharding import PartitionSpec as P

MESH = pl.DeviceIdType.MESH
F32 = jnp.float32

PARTS = {("A", 1): (0, 1792), ("A", 2): (1792, 1792), ("B", 1): (3584, 2304), ("B", 2): (5888, 2304)}
SPAN = {"A": (0, 3584), "B": (3584, 4608)}
RING = 8
CHIPS = 16
LAYERS = 16
N_SEND = 128
N_RECV = 112


def kernel(grads, dec, ids_hbm, act_hbm, out, got, feats, acc, ids, act, picked, r1, half_in, r2, halves,
           send_sem, recv_sem, r1_sem, r2_sem, loc_sem):
    layer = lax.axis_index("layer")
    feat = lax.axis_index("feat")
    core = lax.rem(feat, 2)
    chip = feat // 2
    row = lax.rem(chip, RING)
    side = chip // RING
    other = 1 - core
    rows = grads.shape[2]
    n_feats = dec.shape[2]

    def chip_at(which, off):
        base = side if which == 0 else 1 - side
        return base * RING + lax.rem(row + off + RING, RING)

    def same_core(which, off):
        return {"feat": chip_at(which, off) * 2 + core}

    sibling = {"feat": chip * 2 + other}
    partner = same_core(1, 0)

    local = [
        pltpu.make_async_copy(grads.at[core, 0], got.at[feat], loc_sem.at[0]),
        pltpu.make_async_copy(dec.at[core, 0], feats.at[core], loc_sem.at[1]),
        pltpu.make_async_copy(ids_hbm, ids, loc_sem.at[2]),
        pltpu.make_async_copy(act_hbm, act, loc_sem.at[3]),
    ]
    for copy in local:
        copy.start()

    barrier = pltpu.get_barrier_semaphore()
    peers = [sibling, partner, same_core(0, 1), same_core(0, -1)]
    peers += [{"layer": lax.rem(layer + r, LAYERS)} for r in range(1, LAYERS)]
    for peer in peers:
        pl.semaphore_signal(barrier, inc=1, device_id=peer, device_id_type=MESH)
    pl.semaphore_wait(barrier, len(peers))

    sends = []
    keys = {}

    def sem_of(key):
        return recv_sem.at[keys.setdefault(key, len(keys))]

    def send(src, dst, key, device):
        copy = pltpu.make_async_remote_copy(src, dst, send_sem.at[len(sends)], sem_of(key), device_id=device,
                                            device_id_type=MESH)
        copy.start()
        sends.append(copy)

    def arrive(dst, key):
        pltpu.make_async_remote_copy(dst, dst, send_sem.at[0], sem_of(key), device_id=sibling,
                                     device_id_type=MESH).wait_recv()

    def block(b, typ, part):
        lo, width = PARTS[typ, part]
        return got.at[pl.ds(2 * b, 2), :, pl.ds(lo, width)]

    for typ in ("B", "A"):
        lo, width = SPAN[typ]
        cols = pl.ds(lo, width)
        send(grads.at[other, 0, :, cols], got.at[feat, :, cols], ("swap", typ), sibling)

    def first(src, slot, typ):
        for part in (1, 2):
            lo, width = PARTS[typ, part]
            cols = pl.ds(lo, width)
            for s in (1, -1):
                send(src.at[:, cols], got.at[slot, :, cols], ("y", s, typ, 0, 0, part), same_core(0, s))

    def first_x(src, slot, typ):
        for part in (1, 2):
            lo, width = PARTS[typ, part]
            cols = pl.ds(lo, width)
            send(src.at[:, cols], got.at[slot, :, cols], ("x", typ, 0, part), partner)

    mine = grads.at[core, 0]
    first(mine, feat, "B")
    first_x(mine, feat, "A")
    sib_slot = chip * 2 + other
    sib_rows = got.at[sib_slot]
    for typ, xtyp in (("B", "A"), ("A", "B")):
        lo, width = SPAN[typ]
        if typ == "A":
            first(mine, feat, "A")
            first_x(mine, feat, "B")
            arrive(got.at[sib_slot, :, pl.ds(lo, width)], ("swap", typ))
            first(sib_rows, sib_slot, "A")
            first_x(sib_rows, sib_slot, "A")
            first_x(sib_rows, sib_slot, "B")
        else:
            arrive(got.at[sib_slot, :, pl.ds(lo, width)], ("swap", typ))
            first(sib_rows, sib_slot, "B")
    send(dec.at[other, 0], feats.at[core], ("dec",), sibling)

    def pass_on(typ, which, d):
        for part in (1, 2):
            for s in (1, -1):
                if d == 3 and (part == 1) != (s == 1):
                    continue
                off = -s * (d + 1)
                piece = block(chip_at(which, off), typ, part)
                arrive(piece, ("y", s, typ, which, d, part))
                if d < 2 or (d == 2 and (part == 1) == (s == 1)):
                    send(piece, piece, ("y", s, typ, which, d + 1, part), same_core(0, s))
                if typ == "B":
                    send(piece, piece, ("x", typ, off if d < 3 else 4, part), partner)

    def from_partner(typ, offs):
        for off in offs:
            for part in (1, 2):
                arrive(block(chip_at(1, off), typ, part), ("x", typ, off, part))

    def multiply(blocks, typ, new=False):
        lo, width = SPAN[typ]
        cols = pl.ds(lo, width)
        chips = [chip_at(which, off) for which, off in blocks]
        left = jnp.concatenate([got[pl.ds(2 * b, 2), :, cols].reshape(2 * rows, width) for b in chips], axis=0)
        right = feats[:, :, cols].reshape(2 * n_feats, width)
        part = lax.dot_general(left, right, (((1,), (1,)), ((), ())), preferred_element_type=F32)
        for k, b in enumerate(chips):
            term = part[2 * rows * k: 2 * rows * (k + 1)]
            if new:
                acc[b, :, pl.ds(0, 2 * n_feats)] = term
            else:
                acc[b, :, pl.ds(0, 2 * n_feats)] += term

    layer_sends = []

    def finish(blocks):
        for which, off in blocks:
            b = chip_at(which, off)
            here = ids[pl.ds(pl.multiple_of(2 * rows * b, 2 * rows), 2 * rows), :] - chip * (2 * n_feats)
            lanes = jnp.bitwise_and(here, 127)
            low = jnp.take_along_axis(acc[b, :, pl.ds(0, 128)], lanes, axis=1, mode="promise_in_bounds")
            high = jnp.take_along_axis(acc[b, :, pl.ds(128, 128)], lanes, axis=1, mode="promise_in_bounds")
            value = jnp.where(here < 128, low, high)
            inside = jnp.logical_and(here >= 0, here < 2 * n_feats)
            picked[b] = jnp.where(inside, value, F32(0.0))
            copy = pltpu.make_async_remote_copy(picked.at[b], r1.at[layer], send_sem.at[N_SEND - 1 - len(layer_sends)],
                                                r1_sem.at[layer], device_id={"layer": b}, device_id_type=MESH)
            layer_sends.append((b, copy))

            @pl.when(b != layer)
            def _():
                copy.start()

    acc[...] = jnp.zeros_like(acc)
    near = [(0, 0), (1, 0), (0, 1), (0, -1), (1, 1), (1, -1)]
    two = [(0, 2), (0, -2), (1, 2), (1, -2)]
    three = [(0, 3), (0, -3), (1, 3), (1, -3)]
    four = [(0, 4), (1, 4)]

    pass_on("B", 0, 0)
    for part in (1, 2):
        piece = block(chip_at(1, 0), "A", part)
        arrive(piece, ("x", "A", 0, part))
        for s in (1, -1):
            send(piece, piece, ("y", s, "A", 1, 0, part), same_core(0, s))
    pass_on("A", 0, 0)
    for copy in local:
        copy.wait()
    arrive(feats.at[other], ("dec",))
    pass_on("B", 0, 1)
    pass_on("A", 1, 0)
    multiply(near, "A", True)
    pass_on("A", 0, 1)
    from_partner("B", (0, 1, -1))
    multiply(near, "B")
    finish(near)
    pass_on("B", 0, 2)
    pass_on("A", 1, 1)
    multiply(two, "A", True)
    pass_on("B", 0, 3)
    from_partner("B", (2, -2))
    multiply(two, "B")
    finish(two)
    pass_on("A", 0, 2)
    pass_on("A", 1, 2)
    multiply(three, "A", True)
    from_partner("B", (3, -3))
    multiply(three, "B")
    finish(three)
    pass_on("A", 0, 3)
    pass_on("A", 1, 3)
    multiply(four, "A", True)
    from_partner("B", (4,))
    multiply(four, "B")
    finish(four)

    r1[layer] = picked[layer]
    for r in range(1, LAYERS):
        other_layer = lax.rem(layer + r, LAYERS)
        piece = r1.at[other_layer]
        pltpu.make_async_remote_copy(piece, piece, send_sem.at[0], r1_sem.at[other_layer], device_id=sibling,
                                     device_id_type=MESH).wait_recv()
    total = r1[0]
    for k in range(1, LAYERS):
        total += r1[k]
    halves[0] = total[:rows]
    halves[1] = total[rows:]
    send(halves.at[other], half_in, ("half",), sibling)
    arrive(half_in, ("half",))
    r2[chip] = halves[core] + half_in[...]
    chip_sends = []
    for r in range(1, CHIPS):
        to = lax.rem(chip + r, CHIPS)
        copy = pltpu.make_async_remote_copy(r2.at[chip], r2.at[chip], send_sem.at[N_SEND - 17 - r], r2_sem.at[chip],
                                            device_id={"feat": to * 2 + core}, device_id_type=MESH)
        copy.start()
        chip_sends.append(copy)
    for r in range(1, CHIPS):
        other_chip = lax.rem(chip + r, CHIPS)
        piece = r2.at[other_chip]
        pltpu.make_async_remote_copy(piece, piece, send_sem.at[0], r2_sem.at[other_chip], device_id=sibling,
                                     device_id_type=MESH).wait_recv()
    total = r2[0]
    for k in range(1, CHIPS):
        total += r2[k]
    half_out = halves.at[2 + core]
    halves[2 + core] = total * act[pl.ds(pl.multiple_of(rows * core, rows), rows), :]
    send(half_out, half_out, ("out",), sibling)
    arrive(halves.at[2 + other], ("out",))
    out[pl.ds(0, rows), :] = halves[2]
    out[pl.ds(rows, rows), :] = halves[3]

    for copy in sends + chip_sends:
        copy.wait_send()
    for b, copy in layer_sends:
        @pl.when(b != layer)
        def _():
            copy.wait_send()
    assert len(sends) <= N_SEND - 32 and len(keys) <= N_RECV, (len(sends), len(keys))


def shards(grads, decoder, active_ids, act_vals):
    pairs, _, rows, width = grads.shape
    n_feats = decoder.shape[2]
    tokens, slots = active_ids.shape
    keep = act_vals.shape[0]
    any_spec = pl.BlockSpec(memory_space=pl.ANY)
    return pl.pallas_call(
        kernel,
        name="edges",
        out_shape=jax.ShapeDtypeStruct((keep, slots), F32),
        in_specs=[any_spec] * 4,
        out_specs=pl.BlockSpec(memory_space=pltpu.VMEM),
        scratch_shapes=[
            pltpu.VMEM((2 * CHIPS, rows, width), jnp.bfloat16),
            pltpu.VMEM((2, n_feats, width), jnp.bfloat16),
            pltpu.VMEM((CHIPS, 2 * rows, 256), F32),
            pltpu.VMEM((tokens, slots), jnp.int32),
            pltpu.VMEM((keep, slots), F32),
            pltpu.VMEM((CHIPS, 2 * rows, slots), F32),
            pltpu.VMEM((LAYERS, keep, slots), F32),
            pltpu.VMEM((rows, slots), F32),
            pltpu.VMEM((CHIPS, rows, slots), F32),
            pltpu.VMEM((4, rows, slots), F32),
            pltpu.SemaphoreType.DMA((N_SEND,)),
            pltpu.SemaphoreType.DMA((N_RECV,)),
            pltpu.SemaphoreType.DMA((LAYERS,)),
            pltpu.SemaphoreType.DMA((CHIPS,)),
            pltpu.SemaphoreType.DMA((4,)),
        ],
        compiler_params=pltpu.CompilerParams(collective_id=0, has_side_effects=True, vmem_limit_bytes=48 << 20),
        cost_estimate=pl.CostEstimate(flops=2 * tokens * 2 * n_feats * width, bytes_accessed=4 << 20, transcendentals=0),
    )(grads, decoder, active_ids, act_vals)


def solution(mesh):
    placed = (P(None, "layer", "feat", None), P(None, "layer", "feat", None), P(), P("layer", None))
    return jax.shard_map(
        shards, mesh=mesh, in_specs=placed, out_specs=P("layer", None), check_vma=False
    )
```

time: 288 us -> 70.2 us (0.24)
  waiting for transfers between devices: 174 us -> 0 us
  blocking collectives: 77.9 us -> 0 us
  Pallas kernels: 0 us -> 64.9 us
  between operations: 13.4 us -> 0.01 us
  local copies, waits for them, and re-layouts: 13.8 us -> 5.04 us
  matrix products: 6.37 us -> 0 us
    all_gather x1 -> x0, waiting for transfers between devices: 116 us -> none  [shards(): lax.all_gather(grad_pair, 'feat', axis=1, tiled=True)]
    psum x1 -> x0, blocking collectives: 77.9 us -> none  [finish_scores(): return lax.psum(owned, 'feat')]
    pallas_call x0 -> x1, Pallas kernels: none -> 64.9 us  [shards(): pl.pallas_call(kernel, name='edges', out_shape=jax.ShapeDtypeStruct((keep...]
    reduce_scatter x1 -> x0, waiting for transfers between devices: 57.1 us -> none  [finish_scores(): lax.psum_scatter(partial_scores, 'layer', scatter_dimension=0, tiled=True)]
    gather x1 -> x0, local copies, waits for them, and re-layouts: 13.8 us -> none  [select_owned(): values = jnp.take_along_axis(matrix, safe, axis=1)]
    dot_general x1 -> x0, matrix products: 6.37 us -> none  [shards(): jnp.einsum('ptd,pfd->tf', lax.all_gather(grad_pair, 'feat', axis=1, tiled...]
    unnamed x4 -> x9, local copies, waits for them, and re-layouts: 0.01 us -> 5.04 us
  transfers between devices with their start and end apart: 2 -> 0, of which waited for: 2 -> 0; matrix products, arithmetic and copies ran while one was open for 0% -> 0% of each run, Pallas kernels for 0% -> 0%
where the time goes in v1:
time: 70.2 us; the launch traced here: 70 us
  Pallas kernels  64.9 us (92%)
  local copies, waits for them, and re-layouts  5.04 us (7%)
    pallas_call x1, Pallas kernels, shards(): pl.pallas_call(kernel, name='edges', out_shape=jax.ShapeDtypeStruct((keep...  64.9 us
    unnamed x9, local copies, waits for them, and re-layouts  5.04 us

profile of v1, /device:TPU:1, one launch (start us, length us, event | category | flops | bytes accessed | tf_op | source)
XLA Modules:
  0.0 70.0 jit_solution(14363368782944525684)
XLA Ops:
  0.0 0.0 copy-start
  0.0 1.9 %copy-done = bf16[2,1,96,8192]{3,2,1,0:T(8,128)(2,1)S(1)} copy-done((bf16[2,1,96,8192]{3,2,1,0:T(8,128)(2,1)S(1)}, bf16[2,1,96,8192]{3,2,1,0:T(8,128)(2,1)}, u32[]{:S(2)}) %copy-start) | copy-done | bytes 3145752
  1.9 0.0 copy-start.1
  1.9 0.9 %copy-done.1 = bf16[2,1,8,8192]{3,2,1,0:T(8,128)(2,1)S(1)} copy-done((bf16[2,1,8,8192]{3,2,1,0:T(8,128)(2,1)S(1)}, bf16[2,1,8,8192]{3,2,1,0:T(8,128)(2,1)}, u32[]{:S(2)}) %copy-start.1) | copy-done | bytes 262168
  2.8 0.0 copy-start.2
  2.8 0.9 %copy-done.2 = s32[256,128]{1,0:T(8,128)S(1)} copy-done((s32[256,128]{1,0:T(8,128)S(1)}, s32[256,128]{1,0:T(8,128)}, u32[]{:S(2)}) %copy-start.2) | copy-done | bytes 131096
  3.7 0.0 copy-start.3
  3.7 0.7 copy-done.3
  4.4 64.9 %edges.1 = f32[16,128]{1,0:T(8,128)S(1)} custom-call(bf16[2,1,8,8192]{3,2,1,0:T(8,128)(2,1)S(1)} %copy-done.1, bf16[2,1,96,8192]{3,2,1,0:T(8,128)(2,1)S(1)} %copy-done, s32[256,128]{1,0:T(8,128)S(1)} %copy-done.2, f32[16,128]{1,0:T(8,128)S(1)} %copy-done.3), custom_call_target="tpu_custom_call" | custom-call | flops 805306368 | bytes 4194304 | tf_op jit(solution)/shard_map/edges/pallas_call | solution.py:263
  69.3 0.6 copy.6
Async XLA Ops:
  0.0 1.9 %copy-start = (bf16[2,1,96,8192]{3,2,1,0:T(8,128)(2,1)S(1)}, bf16[2,1,96,8192]{3,2,1,0:T(8,128)(2,1)}, u32[]{:S(2)}) copy-start(bf16[2,1,96,8192]{3,2,1,0:T(8,128)(2,1)} %dec.1) | copy-start | bytes 9437188
  1.9 0.9 %copy-start.1 = (bf16[2,1,8,8192]{3,2,1,0:T(8,128)(2,1)S(1)}, bf16[2,1,8,8192]{3,2,1,0:T(8,128)(2,1)}, u32[]{:S(2)}) copy-start(bf16[2,1,8,8192]{3,2,1,0:T(8,128)(2,1)} %grads.1) | copy-start | bytes 786436
  2.8 0.9 %copy-start.2 = (s32[256,128]{1,0:T(8,128)S(1)}, s32[256,128]{1,0:T(8,128)}, u32[]{:S(2)}) copy-start(s32[256,128]{1,0:T(8,128)} %ids_hbm.1) | copy-start | bytes 393220
  3.7 0.7 copy-start.3

commit v2 on v0

v2 whole, which is shorter than its diff:
```python
import jax
import jax.numpy as jnp
from jax import lax
from jax.experimental import pallas as pl
from jax.experimental.pallas import tpu as pltpu
from jax.sharding import PartitionSpec as P

MESH = pl.DeviceIdType.MESH
F32 = jnp.float32

RING = 8
CHIPS = 16
LAYERS = 16
END = 2560
PARTS = 2


def kernel(grads, dec, ids_hbm, act_hbm, out, got, feats, feats2, acc, acc2, ids, act, picked, r1, r2, half_out,
           send_sem, y_sem, x_sem, pair_sem, dec_sem, r1_sem, r2_sem, out_sem, loc_sem):
    layer = lax.axis_index("layer")
    feat = lax.axis_index("feat")
    core = lax.rem(feat, 2)
    chip = feat // 2
    row = lax.rem(chip, RING)
    side = chip // RING
    other = 1 - core
    rows = grads.shape[2]
    n_feats = dec.shape[2]
    kept = got.shape[2]
    width = kept // PARTS
    shared = kept - END

    def chip_at(which, off):
        base = side if which == 0 else 1 - side
        return base * RING + lax.rem(row + off + RING, RING)

    def device(which, off, c):
        return {"feat": chip_at(which, off) * 2 + c}

    def cols_of(of_side, p=None):
        lo = of_side * END
        if p is None:
            return pl.ds(pl.multiple_of(lo, 128), kept)
        return pl.ds(pl.multiple_of(lo + p * width, 128), width)

    def end_of(of_side):
        return pl.ds(pl.multiple_of(of_side * (END + shared), 128), END)

    sibling = device(0, 0, other)

    local = [
        pltpu.make_async_copy(grads.at[core, 0, :, cols_of(side)], got.at[feat], loc_sem.at[0]),
        pltpu.make_async_copy(dec.at[core, 0, :, cols_of(side)], feats.at[core], loc_sem.at[1]),
        pltpu.make_async_copy(ids_hbm, ids, loc_sem.at[2]),
        pltpu.make_async_copy(act_hbm, act, loc_sem.at[3]),
    ]

    barrier = pltpu.get_barrier_semaphore()
    peers = [device(0, s, c) for s in (1, -1) for c in (core, other)]
    peers += [device(1, 0, core), device(1, 0, other), sibling]
    for r in range(1, LAYERS):
        peers += [{"layer": lax.rem(layer + r, LAYERS), "feat": chip * 2 + c} for c in (core, other)]
    for peer in peers:
        pl.semaphore_signal(barrier, inc=1, device_id=peer, device_id_type=MESH)
    for copy in local:
        copy.start()
    pl.semaphore_wait(barrier, len(peers))

    def remote(src, dst, sem, to, out_at=0):
        return pltpu.make_async_remote_copy(src, dst, send_sem.at[out_at], sem, device_id=to, device_id_type=MESH)

    def send(src, dst, sem, to, out_at=0):
        remote(src, dst, sem, to, out_at).start()

    def sent(as_much_as, out_at):
        remote(as_much_as, as_much_as, send_sem.at[out_at], sibling, out_at).wait_send()

    def arrive(dst, sem):
        pltpu.make_async_remote_copy(dst, dst, send_sem.at[0], sem, device_id=sibling, device_id_type=MESH).wait_recv()

    def piece_of(b, p):
        return got.at[pl.ds(2 * b, 2), :, pl.ds(p * width, width)]

    def y_at(back, which, d, p):
        steps = 3 * PARTS + PARTS // 2
        return y_sem.at[back, which * steps + d * PARTS + (p if d < 3 else p % (PARTS // 2))]

    for p in range(PARTS):
        dst = got.at[feat, :, pl.ds(p * width, width)]
        for c in (core, other):
            for back, s in ((0, 1), (1, -1)):
                send(grads.at[c, 0, :, cols_of(side, p)], dst, y_at(back, 0, 0, p), device(0, s, c))
            send(grads.at[c, 0, :, cols_of(1 - side, p)], dst, x_sem.at[p], device(1, 0, c))
    send(grads.at[other, 0, :, cols_of(side)], got.at[feat], pair_sem.at[0], sibling)
    send(dec.at[other, 0, :, cols_of(side)], feats.at[core], pair_sem.at[1], sibling, 1)
    for c in (core, other):
        send(dec.at[c, 0, :, end_of(1 - side)], feats2.at[core], dec_sem.at[core], device(1, 0, c), 2)

    def joins(p):
        piece = piece_of(chip_at(1, 0), p)
        arrive(piece, x_sem.at[p])
        for back, s in ((0, 1), (1, -1)):
            send(piece, piece, y_at(back, 1, 0, p), device(0, s, core))

    def pass_on(which, d, p):
        for back, s in ((0, 1), (1, -1)):
            q = p if back == 0 or d == 0 else PARTS - 1 - p
            if d == 3 and p >= PARTS // 2:
                continue
            piece = piece_of(chip_at(which, -s * (d + 1)), q)
            arrive(piece, y_at(back, which, d, q))
            if d < 2 or (d == 2 and p < PARTS // 2):
                send(piece, piece, y_at(back, which, d + 1, q), device(0, s, core))

    def multiply(blocks):
        chips = [chip_at(which, off) for which, off in blocks]
        left = jnp.concatenate([got[pl.ds(2 * b, 2)].reshape(2 * rows, kept) for b in chips], axis=0)
        right = feats[...].reshape(2 * n_feats, kept)
        part = lax.dot_general(left, right, (((1,), (1,)), ((), ())), preferred_element_type=F32)
        for k, b in enumerate(chips):
            acc[b, :, pl.ds(0, 2 * n_feats)] = part[2 * rows * k: 2 * rows * (k + 1)]

    def multiply2(blocks):
        cols = pl.ds(pl.multiple_of(side * shared, 128), END)
        chips = [chip_at(which, off) for which, off in blocks]
        left = jnp.concatenate([got[pl.ds(2 * b, 2), :, cols].reshape(2 * rows, END) for b in chips], axis=0)
        right = feats2[...].reshape(2 * n_feats, END)
        part = lax.dot_general(left, right, (((1,), (1,)), ((), ())), preferred_element_type=F32)
        for k, b in enumerate(chips):
            acc2[b, :, pl.ds(0, 2 * n_feats)] = part[2 * rows * k: 2 * rows * (k + 1)]

    def pick(table, b, here):
        lanes = jnp.bitwise_and(here, 127)
        low = jnp.take_along_axis(table[b, :, pl.ds(0, 128)], lanes, axis=1, mode="promise_in_bounds")
        high = jnp.take_along_axis(table[b, :, pl.ds(128, 128)], lanes, axis=1, mode="promise_in_bounds")
        inside = jnp.logical_and(here >= 0, here < 2 * n_feats)
        return jnp.where(inside, jnp.where(here < 128, low, high), F32(0.0))

    def finish(blocks):
        for which, off in blocks:
            b = chip_at(which, off)
            named = ids[pl.ds(pl.multiple_of(2 * rows * b, 2 * rows), 2 * rows), :]
            value = pick(acc, b, named - chip * (2 * n_feats)) + pick(acc2, b, named - chip_at(1, 0) * (2 * n_feats))
            picked[b, 0] = value[:rows]
            picked[b, 1] = value[rows:]
            away = b != layer
            for c in (other, core):
                copy = remote(picked.at[b, c], r1.at[layer * 2 + core], r1_sem.at[0], {"layer": b, "feat": chip * 2 + c}, 3)
                if c is other:
                    copy.start()
                else:
                    pl.when(away)(copy.start)

    acc[...] = jnp.zeros_like(acc)
    acc2[...] = jnp.zeros_like(acc2)
    near = [(0, 0), (1, 0), (0, 1), (0, -1), (1, 1), (1, -1)]
    two = [(0, 2), (0, -2), (1, 2), (1, -2)]
    three = [(0, 3), (0, -3), (1, 3), (1, -3)]
    four = [(0, 4), (1, 4)]

    def step(which, d):
        for p in range(PARTS):
            pass_on(which, d, p)

    step(0, 0)
    for p in range(PARTS):
        joins(p)
    for copy in local:
        copy.wait()
    arrive(got.at[chip * 2 + other], pair_sem.at[0])
    arrive(feats.at[other], pair_sem.at[1])
    step(0, 1)
    step(1, 0)
    multiply(near)
    step(0, 2)
    step(1, 1)
    multiply(two)
    step(0, 3)
    step(1, 2)
    multiply(three)
    for c in (core, other):
        arrive(feats2.at[c], dec_sem.at[c])
    for blocks in (near, two, three):
        multiply2(blocks)
        finish(blocks)
    step(1, 3)
    multiply(four)
    multiply2(four)
    finish(four)

    r1[layer * 2 + core] = picked[layer, core]
    from_layers = r1.at[pl.ds(0, 2 * LAYERS - 1)]
    arrive(from_layers, r1_sem.at[0])
    total = r1[0]
    for k in range(1, 2 * LAYERS):
        total += r1[k]
    r2[chip] = total
    far_first = sorted([(which, off) for which in (0, 1) for off in range(RING) if (which, off) != (0, 0)],
                       key=lambda m: -(2 * m[0] + min(m[1], RING - m[1])))
    for which, off in far_first:
        send(r2.at[chip], r2.at[chip], r2_sem.at[0], device(which, off, core), 4)
    from_chips = r2.at[pl.ds(0, CHIPS - 1)]
    arrive(from_chips, r2_sem.at[0])
    total = r2[0]
    for k in range(1, CHIPS):
        total += r2[k]
    half_out[...] = total * act[pl.ds(pl.multiple_of(rows * core, rows), rows), :]
    to_out = out.at[pl.ds(pl.multiple_of(rows * core, rows), rows), :]
    send(half_out, to_out, out_sem.at[0], sibling, 5)
    own_out = pltpu.make_async_copy(half_out, to_out, loc_sem.at[4])
    own_out.start()

    sent(got.at[pl.ds(0, 31)], 0)
    sent(feats.at[0], 1)
    sent(feats2, 2)
    sent(from_layers, 3)
    sent(from_chips, 4)
    sent(half_out, 5)
    own_out.wait()
    arrive(out.at[pl.ds(pl.multiple_of(rows * other, rows), rows), :], out_sem.at[0])


def shards(grads, decoder, active_ids, act_vals):
    pairs, _, rows, width = grads.shape
    n_feats = decoder.shape[2]
    tokens, slots = active_ids.shape
    keep = act_vals.shape[0]
    kept = width - END
    any_spec = pl.BlockSpec(memory_space=pl.ANY)
    return pl.pallas_call(
        kernel,
        name="edges",
        out_shape=jax.ShapeDtypeStruct((keep, slots), F32),
        in_specs=[any_spec] * 4,
        out_specs=any_spec,
        scratch_shapes=[
            pltpu.VMEM((2 * CHIPS, rows, kept), jnp.bfloat16),
            pltpu.VMEM((2, n_feats, kept), jnp.bfloat16),
            pltpu.VMEM((2, n_feats, END), jnp.bfloat16),
            pltpu.VMEM((CHIPS, 2 * rows, 256), F32),
            pltpu.VMEM((CHIPS, 2 * rows, 256), F32),
            pltpu.VMEM((tokens, slots), jnp.int32),
            pltpu.VMEM((keep, slots), F32),
            pltpu.VMEM((CHIPS, 2, rows, slots), F32),
            pltpu.VMEM((2 * LAYERS, rows, slots), F32),
            pltpu.VMEM((CHIPS, rows, slots), F32),
            pltpu.VMEM((rows, slots), F32),
            pltpu.SemaphoreType.DMA((6,)),
            pltpu.SemaphoreType.DMA((2, 7 * PARTS)),
            pltpu.SemaphoreType.DMA((PARTS,)),
            pltpu.SemaphoreType.DMA((2,)),
            pltpu.SemaphoreType.DMA((2,)),
            pltpu.SemaphoreType.DMA((1,)),
            pltpu.SemaphoreType.DMA((1,)),
            pltpu.SemaphoreType.DMA((1,)),
            pltpu.SemaphoreType.DMA((5,)),
        ],
        compiler_params=pltpu.CompilerParams(collective_id=0, has_side_effects=True, vmem_limit_bytes=60 << 20),
        cost_estimate=pl.CostEstimate(flops=2 * tokens * 2 * n_feats * width, bytes_accessed=4 << 20, transcendentals=0),
    )(grads, decoder, active_ids, act_vals)


def solution(mesh):
    placed = (P(None, "layer", "feat", None), P(None, "layer", "feat", None), P(), P("layer", None))
    return jax.shard_map(
        shards, mesh=mesh, in_specs=placed, out_specs=P("layer", None), check_vma=False
    )
```

time: 288 us -> 63.4 us (0.22)
  waiting for transfers between devices: 174 us -> 0 us
  blocking collectives: 77.9 us -> 0 us
  Pallas kernels: 0 us -> 62 us
  between operations: 13.4 us -> 0.01 us
  local copies, waits for them, and re-layouts: 13.8 us -> 1.3 us
  matrix products: 6.37 us -> 0 us
    all_gather x1 -> x0, waiting for transfers between devices: 116 us -> none  [shards(): lax.all_gather(grad_pair, 'feat', axis=1, tiled=True)]
    psum x1 -> x0, blocking collectives: 77.9 us -> none  [finish_scores(): return lax.psum(owned, 'feat')]
    pallas_call x0 -> x1, Pallas kernels: none -> 62 us  [shards(): pl.pallas_call(kernel, name='edges', out_shape=jax.ShapeDtypeStruct((keep...]
    reduce_scatter x1 -> x0, waiting for transfers between devices: 57.1 us -> none  [finish_scores(): lax.psum_scatter(partial_scores, 'layer', scatter_dimension=0, tiled=True)]
    gather x1 -> x0, local copies, waits for them, and re-layouts: 13.8 us -> none  [select_owned(): values = jnp.take_along_axis(matrix, safe, axis=1)]
    dot_general x1 -> x0, matrix products: 6.37 us -> none  [shards(): jnp.einsum('ptd,pfd->tf', lax.all_gather(grad_pair, 'feat', axis=1, tiled...]
  transfers between devices with their start and end apart: 2 -> 0, of which waited for: 2 -> 0; matrix products, arithmetic and copies ran while one was open for 0% -> 0% of each run, Pallas kernels for 0% -> 0%
where the time goes in v2:
time: 63.4 us; the launch traced here: 63.3 us
  Pallas kernels  62 us (98%)
  local copies, waits for them, and re-layouts  1.3 us (2%)
    pallas_call x1, Pallas kernels, shards(): pl.pallas_call(kernel, name='edges', out_shape=jax.ShapeDtypeStruct((keep...  62 us
    unnamed x1, local copies, waits for them, and re-layouts  1.3 us

profile of v2, /device:TPU:1, one launch (start us, length us, event | category | flops | bytes accessed | tf_op | source)
XLA Modules:
  0.0 63.3 jit_solution(5594986058328938475)
XLA Ops:
  0.0 62.0 %edges.1 = f32[16,128]{1,0:T(8,128)} custom-call(bf16[2,1,8,8192]{3,2,1,0:T(8,128)(2,1)} %grads.1, bf16[2,1,96,8192]{3,2,1,0:T(8,128)(2,1)} %dec.1, s32[256,128]{1,0:T(8,128)} %ids_hbm.1, f32[16,128]{1,0:T(8,128)} %act_hbm.1), custom_call_target="tpu_custom_call" | custom-call | flops 805306368 | bytes 4194304 | tf_op jit(solution)/shard_map/edges/pallas_call | solution.py:230
  62.0 1.3 %copy.6 = f32[16,128]{1,0:T(8,128)} copy(f32[16,128]{1,0:T(8,128)} %edges.1) | data formatting | bytes 16384

commit v3 on v2

--- a/solution.py
+++ b/solution.py
@@ -11,12 +11,14 @@
 RING = 8
 CHIPS = 16
 LAYERS = 16
-END = 2560
+END = 2816
+CHUNKS = ((0, 2304), (2304, 512))
 PARTS = 2
-
-
-def kernel(grads, dec, ids_hbm, act_hbm, out, got, feats, feats2, acc, acc2, ids, act, picked, r1, r2, half_out,
-           send_sem, y_sem, x_sem, pair_sem, dec_sem, r1_sem, r2_sem, out_sem, loc_sem):
+VMEM_LIMIT = 55193 << 10
+
+
+def kernel(grads, dec, ids_hbm, out, own, got, feats, feats2, acc, acc2, ids, picked, r1, r2, whole,
+           send_sem, y_sem, x_sem, pair_sem, dec_sem, r1_sem, r2_sem, loc_sem):
     layer = lax.axis_index("layer")
     feat = lax.axis_index("feat")
     core = lax.rem(feat, 2)
@@ -43,17 +45,14 @@
             return pl.ds(pl.multiple_of(lo, 128), kept)
         return pl.ds(pl.multiple_of(lo + p * width, 128), width)
 
-    def end_of(of_side):
-        return pl.ds(pl.multiple_of(of_side * (END + shared), 128), END)
-
     sibling = device(0, 0, other)
 
     local = [
         pltpu.make_async_copy(grads.at[core, 0, :, cols_of(side)], got.at[feat], loc_sem.at[0]),
         pltpu.make_async_copy(dec.at[core, 0, :, cols_of(side)], feats.at[core], loc_sem.at[1]),
         pltpu.make_async_copy(ids_hbm, ids, loc_sem.at[2]),
-        pltpu.make_async_copy(act_hbm, act, loc_sem.at[3]),
     ]
+    own_rows = pltpu.make_async_copy(grads.at[:, 0], own, loc_sem.at[5])
 
     barrier = pltpu.get_barrier_semaphore()
     peers = [device(0, s, c) for s in (1, -1) for c in (core, other)]
@@ -62,9 +61,11 @@
         peers += [{"layer": lax.rem(layer + r, LAYERS), "feat": chip * 2 + c} for c in (core, other)]
     for peer in peers:
         pl.semaphore_signal(barrier, inc=1, device_id=peer, device_id_type=MESH)
+    own_rows.start()
     for copy in local:
         copy.start()
     pl.semaphore_wait(barrier, len(peers))
+    own_rows.wait()
 
     def remote(src, dst, sem, to, out_at=0):
         return pltpu.make_async_remote_copy(src, dst, send_sem.at[out_at], sem, device_id=to, device_id_type=MESH)
@@ -89,12 +90,14 @@
         dst = got.at[feat, :, pl.ds(p * width, width)]
         for c in (core, other):
             for back, s in ((0, 1), (1, -1)):
-                send(grads.at[c, 0, :, cols_of(side, p)], dst, y_at(back, 0, 0, p), device(0, s, c))
-            send(grads.at[c, 0, :, cols_of(1 - side, p)], dst, x_sem.at[p], device(1, 0, c))
-    send(grads.at[other, 0, :, cols_of(side)], got.at[feat], pair_sem.at[0], sibling)
+                send(own.at[c, :, cols_of(side, p)], dst, y_at(back, 0, 0, p), device(0, s, c))
+            send(own.at[c, :, cols_of(1 - side, p)], dst, x_sem.at[p], device(1, 0, c))
+    send(own.at[other, :, cols_of(side)], got.at[feat], pair_sem.at[0], sibling)
     send(dec.at[other, 0, :, cols_of(side)], feats.at[core], pair_sem.at[1], sibling, 1)
-    for c in (core, other):
-        send(dec.at[c, 0, :, end_of(1 - side)], feats2.at[core], dec_sem.at[core], device(1, 0, c), 2)
+    for k, (lo, size) in enumerate(CHUNKS):
+        for c in (core, other):
+            theirs = pl.ds(pl.multiple_of((1 - side) * (END + shared) + lo, 128), size)
+            send(dec.at[c, 0, :, theirs], feats2.at[core, :, pl.ds(lo, size)], dec_sem.at[k], device(1, 0, c), 2)
 
     def joins(p):
         piece = piece_of(chip_at(1, 0), p)
@@ -120,14 +123,23 @@
         for k, b in enumerate(chips):
             acc[b, :, pl.ds(0, 2 * n_feats)] = part[2 * rows * k: 2 * rows * (k + 1)]
 
-    def multiply2(blocks):
-        cols = pl.ds(pl.multiple_of(side * shared, 128), END)
+    def multiply2(blocks, k):
+        lo, size = CHUNKS[k]
+        cols = pl.ds(pl.multiple_of(side * shared + lo, 128), size)
         chips = [chip_at(which, off) for which, off in blocks]
-        left = jnp.concatenate([got[pl.ds(2 * b, 2), :, cols].reshape(2 * rows, END) for b in chips], axis=0)
-        right = feats2[...].reshape(2 * n_feats, END)
+        left = jnp.concatenate([got[pl.ds(2 * b, 2), :, cols].reshape(2 * rows, size) for b in chips], axis=0)
+        right = feats2[:, :, pl.ds(lo, size)].reshape(2 * n_feats, size)
         part = lax.dot_general(left, right, (((1,), (1,)), ((), ())), preferred_element_type=F32)
-        for k, b in enumerate(chips):
-            acc2[b, :, pl.ds(0, 2 * n_feats)] = part[2 * rows * k: 2 * rows * (k + 1)]
+        for i, b in enumerate(chips):
+            term = part[2 * rows * i: 2 * rows * (i + 1)]
+            if k == 0:
+                acc2[b, :, pl.ds(0, 2 * n_feats)] = term
+            else:
+                acc2[b, :, pl.ds(0, 2 * n_feats)] += term
+
+    def end_rows(k):
+        lo, size = CHUNKS[k]
+        arrive(feats2.at[:, :, pl.ds(lo, size)], dec_sem.at[k])
 
     def pick(table, b, here):
         lanes = jnp.bitwise_and(here, 127)
@@ -177,15 +189,17 @@
     multiply(two)
     step(0, 3)
     step(1, 2)
+    end_rows(0)
+    multiply2(near + two, 0)
     multiply(three)
-    for c in (core, other):
-        arrive(feats2.at[c], dec_sem.at[c])
-    for blocks in (near, two, three):
-        multiply2(blocks)
-        finish(blocks)
+    multiply2(three, 0)
+    end_rows(1)
+    multiply2(near + two + three, 1)
+    finish(near + two + three)
     step(1, 3)
     multiply(four)
-    multiply2(four)
+    multiply2(four, 0)
+    multiply2(four, 1)
     finish(four)
 
     r1[layer * 2 + core] = picked[layer, core]
@@ -194,20 +208,22 @@
     total = r1[0]
     for k in range(1, 2 * LAYERS):
         total += r1[k]
-    r2[chip] = total
-    far_first = sorted([(which, off) for which in (0, 1) for off in range(RING) if (which, off) != (0, 0)],
+    mine = chip * 2 + core
+    r2[mine] = total
+    far_first = sorted([(which, off) for which in (0, 1) for off in range(RING)],
                        key=lambda m: -(2 * m[0] + min(m[1], RING - m[1])))
     for which, off in far_first:
-        send(r2.at[chip], r2.at[chip], r2_sem.at[0], device(which, off, core), 4)
-    from_chips = r2.at[pl.ds(0, CHIPS - 1)]
+        for c in (other, core):
+            if (which, off) != (0, 0) or c is other:
+                send(r2.at[mine], r2.at[mine], r2_sem.at[0], device(which, off, c), 4)
+    from_chips = r2.at[pl.ds(0, 2 * CHIPS - 1)]
     arrive(from_chips, r2_sem.at[0])
-    total = r2[0]
-    for k in range(1, CHIPS):
-        total += r2[k]
-    half_out[...] = total * act[pl.ds(pl.multiple_of(rows * core, rows), rows), :]
-    to_out = out.at[pl.ds(pl.multiple_of(rows * core, rows), rows), :]
-    send(half_out, to_out, out_sem.at[0], sibling, 5)
-    own_out = pltpu.make_async_copy(half_out, to_out, loc_sem.at[4])
+    for c in (0, 1):
+        total = r2[c]
+        for k in range(1, CHIPS):
+            total += r2[2 * k + c]
+        whole[pl.ds(rows * c, rows), :] = total
+    own_out = pltpu.make_async_copy(whole, out, loc_sem.at[4])
     own_out.start()
 
     sent(got.at[pl.ds(0, 31)], 0)
@@ -215,9 +231,7 @@
     sent(feats2, 2)
     sent(from_layers, 3)
     sent(from_chips, 4)
-    sent(half_out, 5)
     own_out.wait()
-    arrive(out.at[pl.ds(pl.multiple_of(rows * other, rows), rows), :], out_sem.at[0])
 
 
 def shards(grads, decoder, active_ids, act_vals):
@@ -231,20 +245,20 @@
         kernel,
         name="edges",
         out_shape=jax.ShapeDtypeStruct((keep, slots), F32),
-        in_specs=[any_spec] * 4,
+        in_specs=[any_spec] * 3,
         out_specs=any_spec,
         scratch_shapes=[
+            pltpu.VMEM((pairs, rows, width), jnp.bfloat16),
             pltpu.VMEM((2 * CHIPS, rows, kept), jnp.bfloat16),
             pltpu.VMEM((2, n_feats, kept), jnp.bfloat16),
             pltpu.VMEM((2, n_feats, END), jnp.bfloat16),
             pltpu.VMEM((CHIPS, 2 * rows, 256), F32),
             pltpu.VMEM((CHIPS, 2 * rows, 256), F32),
             pltpu.VMEM((tokens, slots), jnp.int32),
-            pltpu.VMEM((keep, slots), F32),
             pltpu.VMEM((CHIPS, 2, rows, slots), F32),
             pltpu.VMEM((2 * LAYERS, rows, slots), F32),
-            pltpu.VMEM((CHIPS, rows, slots), F32),
-            pltpu.VMEM((rows, slots), F32),
+            pltpu.VMEM((2 * CHIPS, rows, slots), F32),
+            pltpu.VMEM((keep, slots), F32),
             pltpu.SemaphoreType.DMA((6,)),
             pltpu.SemaphoreType.DMA((2, 7 * PARTS)),
             pltpu.SemaphoreType.DMA((PARTS,)),
@@ -252,12 +266,11 @@
             pltpu.SemaphoreType.DMA((2,)),
             pltpu.SemaphoreType.DMA((1,)),
             pltpu.SemaphoreType.DMA((1,)),
-            pltpu.SemaphoreType.DMA((1,)),
-            pltpu.SemaphoreType.DMA((5,)),
+            pltpu.SemaphoreType.DMA((6,)),
         ],
-        compiler_params=pltpu.CompilerParams(collective_id=0, has_side_effects=True, vmem_limit_bytes=60 << 20),
+        compiler_params=pltpu.CompilerParams(collective_id=0, has_side_effects=True, vmem_limit_bytes=VMEM_LIMIT),
         cost_estimate=pl.CostEstimate(flops=2 * tokens * 2 * n_feats * width, bytes_accessed=4 << 20, transcendentals=0),
-    )(grads, decoder, active_ids, act_vals)
+    )(grads, decoder, active_ids) * act_vals
 
 
 def solution(mesh):

time: 63.4 us -> 59.8 us (0.943)
  Pallas kernels: 62 us -> 59.1 us
  local copies, waits for them, and re-layouts: 1.3 us -> 0.01 us
    pallas_call x1, Pallas kernels: 62 us -> 59.1 us  [shards(): pl.pallas_call(kernel, name='edges', out_shape=jax.ShapeDtypeStruct((keep...]
    unnamed x1 -> x2, local copies, waits for them, and re-layouts: 1.3 us -> 0.01 us
where the time goes in v3:
time: 59.8 us; the launch traced here: 59.7 us
  Pallas kernels  59.1 us (99%)
  other arithmetic  0.6 us (1%)
    pallas_call x1, Pallas kernels, shards(): pl.pallas_call(kernel, name='edges', out_shape=jax.ShapeDtypeStruct((keep...  59.1 us

profile of v3, /device:TPU:1, one launch (start us, length us, event | category | flops | bytes accessed | tf_op | source)
XLA Modules:
  0.0 59.7 jit_solution(12905741891726436297)
XLA Ops:
  0.0 0.0 copy-start
  0.0 59.1 %edges.1 = f32[16,128]{1,0:T(8,128)S(1)} custom-call(bf16[2,1,8,8192]{3,2,1,0:T(8,128)(2,1)} %grads.1, bf16[2,1,96,8192]{3,2,1,0:T(8,128)(2,1)} %dec.1, s32[256,128]{1,0:T(8,128)} %ids_hbm.1), custom_call_target="tpu_custom_call" | custom-call | flops 805306368 | bytes 4194304 | tf_op jit(solution)/shard_map/edges/pallas_call | solution.py:244
  59.1 0.0 copy-done
  59.1 0.6 %mul.3 = f32[16,128]{1,0:T(8,128)} multiply(f32[16,128]{1,0:T(8,128)S(1)} %edges.1, f32[16,128]{1,0:T(8,128)S(1)} %copy-done) | non-fusion elementwise | flops 2048 | bytes 24576 | tf_op jit(solution)/shard_map/mul | solution.py:244
Async XLA Ops:
  0.0 59.1 %copy-start = (f32[16,128]{1,0:T(8,128)S(1)}, f32[16,128]{1,0:T(8,128)}, u32[]{:S(2)}) copy-start(f32[16,128]{1,0:T(8,128)} %param.7) | copy-start | bytes 24580

commit v4 on v3

--- a/solution.py
+++ b/solution.py
@@ -17,8 +17,8 @@
 VMEM_LIMIT = 55193 << 10
 
 
-def kernel(grads, dec, ids_hbm, out, own, got, feats, feats2, acc, acc2, ids, picked, r1, r2, whole,
-           send_sem, y_sem, x_sem, pair_sem, dec_sem, r1_sem, r2_sem, loc_sem):
+def kernel(grads, dec, ids_hbm, out, own, got, feats, feats2, acc, acc2, ids, picked, from_pair, both, r1, r2, whole,
+           send_sem, y_sem, x_sem, pair_sem, dec_sem, r1_sem, r2_sem, half_sem, loc_sem):
     layer = lax.axis_index("layer")
     feat = lax.axis_index("feat")
     core = lax.rem(feat, 2)
@@ -57,8 +57,7 @@
     barrier = pltpu.get_barrier_semaphore()
     peers = [device(0, s, c) for s in (1, -1) for c in (core, other)]
     peers += [device(1, 0, core), device(1, 0, other), sibling]
-    for r in range(1, LAYERS):
-        peers += [{"layer": lax.rem(layer + r, LAYERS), "feat": chip * 2 + c} for c in (core, other)]
+    peers += [{"layer": lax.rem(layer + r, LAYERS)} for r in range(1, LAYERS)]
     for peer in peers:
         pl.semaphore_signal(barrier, inc=1, device_id=peer, device_id_type=MESH)
     own_rows.start()
@@ -148,20 +147,29 @@
         inside = jnp.logical_and(here >= 0, here < 2 * n_feats)
         return jnp.where(inside, jnp.where(here < 128, low, high), F32(0.0))
 
-    def finish(blocks):
-        for which, off in blocks:
+    def choose(blocks, at):
+        for k, (which, off) in enumerate(blocks):
             b = chip_at(which, off)
             named = ids[pl.ds(pl.multiple_of(2 * rows * b, 2 * rows), 2 * rows), :]
             value = pick(acc, b, named - chip * (2 * n_feats)) + pick(acc2, b, named - chip_at(1, 0) * (2 * n_feats))
-            picked[b, 0] = value[:rows]
-            picked[b, 1] = value[rows:]
+            picked[0, at + k] = value[:rows]
+            picked[1, at + k] = value[rows:]
+        span = pl.ds(at, len(blocks))
+        send(picked.at[other, span], from_pair.at[span], half_sem.at[0 if at == 0 else 1], sibling, 5)
+
+    def finish(blocks, at):
+        span = pl.ds(at, len(blocks))
+        arrive(from_pair.at[span], half_sem.at[0 if at == 0 else 1])
+        for k, (which, off) in enumerate(blocks):
+            b = chip_at(which, off)
+            both[at + k] = picked[core, at + k] + from_pair[at + k]
+            copy = remote(both.at[at + k], r1.at[layer], r1_sem.at[0], {"layer": b}, 3)
             away = b != layer
-            for c in (other, core):
-                copy = remote(picked.at[b, c], r1.at[layer * 2 + core], r1_sem.at[0], {"layer": b, "feat": chip * 2 + c}, 3)
-                if c is other:
-                    copy.start()
-                else:
-                    pl.when(away)(copy.start)
+            pl.when(away)(copy.start)
+
+            @pl.when(jnp.logical_not(away))
+            def _():
+                r1[layer] = both[at + k]
 
     acc[...] = jnp.zeros_like(acc)
     acc2[...] = jnp.zeros_like(acc2)
@@ -193,20 +201,22 @@
     multiply2(near + two, 0)
     multiply(three)
     multiply2(three, 0)
+    early = near + two + three
     end_rows(1)
-    multiply2(near + two + three, 1)
-    finish(near + two + three)
+    multiply2(early, 1)
+    choose(early, 0)
     step(1, 3)
     multiply(four)
+    finish(early, 0)
     multiply2(four, 0)
     multiply2(four, 1)
-    finish(four)
-
-    r1[layer * 2 + core] = picked[layer, core]
-    from_layers = r1.at[pl.ds(0, 2 * LAYERS - 1)]
+    choose(four, len(early))
+    finish(four, len(early))
+
+    from_layers = r1.at[pl.ds(0, LAYERS - 1)]
     arrive(from_layers, r1_sem.at[0])
     total = r1[0]
-    for k in range(1, 2 * LAYERS):
+    for k in range(1, LAYERS):
         total += r1[k]
     mine = chip * 2 + core
     r2[mine] = total
@@ -231,6 +241,7 @@
     sent(feats2, 2)
     sent(from_layers, 3)
     sent(from_chips, 4)
+    sent(from_pair, 5)
     own_out.wait()
 
 
@@ -255,8 +266,10 @@
             pltpu.VMEM((CHIPS, 2 * rows, 256), F32),
             pltpu.VMEM((CHIPS, 2 * rows, 256), F32),
             pltpu.VMEM((tokens, slots), jnp.int32),
-            pltpu.VMEM((CHIPS, 2, rows, slots), F32),
-            pltpu.VMEM((2 * LAYERS, rows, slots), F32),
+            pltpu.VMEM((2, CHIPS, rows, slots), F32),
+            pltpu.VMEM((CHIPS, rows, slots), F32),
+            pltpu.VMEM((CHIPS, rows, slots), F32),
+            pltpu.VMEM((LAYERS, rows, slots), F32),
             pltpu.VMEM((2 * CHIPS, rows, slots), F32),
             pltpu.VMEM((keep, slots), F32),
             pltpu.SemaphoreType.DMA((6,)),
@@ -266,6 +279,7 @@
             pltpu.SemaphoreType.DMA((2,)),
             pltpu.SemaphoreType.DMA((1,)),
             pltpu.SemaphoreType.DMA((1,)),
+            pltpu.SemaphoreType.DMA((2,)),
             pltpu.SemaphoreType.DMA((6,)),
         ],
         compiler_params=pltpu.CompilerParams(collective_id=0, has_side_effects=True, vmem_limit_bytes=VMEM_LIMIT),

time: 59.8 us -> 59.6 us (level)
  no operation moved by 1% of the time
where the time goes in v4:
time: 59.6 us; the launch traced here: 59.5 us
  Pallas kernels  58.8 us (99%)
  other arithmetic  0.6 us (1%)
    pallas_call x1, Pallas kernels, shards(): pl.pallas_call(kernel, name='edges', out_shape=jax.ShapeDtypeStruct((keep...  58.8 us

profile of v4, /device:TPU:1, one launch (start us, length us, event | category | flops | bytes accessed | tf_op | source)
XLA Modules:
  0.0 59.5 jit_solution(17708597671129114432)
XLA Ops:
  0.0 0.0 copy-start
  0.0 58.8 %edges.1 = f32[16,128]{1,0:T(8,128)S(1)} custom-call(bf16[2,1,8,8192]{3,2,1,0:T(8,128)(2,1)} %grads.1, bf16[2,1,96,8192]{3,2,1,0:T(8,128)(2,1)} %dec.1, s32[256,128]{1,0:T(8,128)} %ids_hbm.1), custom_call_target="tpu_custom_call" | custom-call | flops 805306368 | bytes 4194304 | tf_op jit(solution)/shard_map/edges/pallas_call | solution.py:255
  58.8 0.0 copy-done
  58.8 0.6 %mul.3 = f32[16,128]{1,0:T(8,128)} multiply(f32[16,128]{1,0:T(8,128)S(1)} %edges.1, f32[16,128]{1,0:T(8,128)S(1)} %copy-done) | non-fusion elementwise | flops 2048 | bytes 24576 | tf_op jit(solution)/shard_map/mul | solution.py:255
Async XLA Ops:
  0.0 58.8 %copy-start = (f32[16,128]{1,0:T(8,128)S(1)}, f32[16,128]{1,0:T(8,128)}, u32[]{:S(2)}) copy-start(f32[16,128]{1,0:T(8,128)} %param.7) | copy-start | bytes 24580
